TPU v7x, 512 devices: a whole 4x8x8 slice. The times are simulated.
512 devices in a mesh: dp: 4 (over y_lo), seq: 16 (over x, y_hi, core), tensor: 8 (over z).
Axes of the slice: x: 4, y: 8 (y_hi: 2, y_lo: 4; y = y_hi * 4 + y_lo), z: 8, core: 2. Of those that a mesh axis runs over, the one named last changes fastest.
Arguments:
- tokens: bfloat16 [4096, 4096], P(('dp', 'seq')), parts along dimension 0, may hold values from -6 to 6
- gate_codes: bfloat16 [14336, 4096], P(('seq', 'tensor')), may hold values from -8 to 7, as said below
- gate_scales: float32 [14336, 32], P(('seq', 'tensor')), may hold values from 0.00125 to 0.00625
- up_codes: bfloat16 [14336, 4096], P(('seq', 'tensor')), may hold values from -8 to 7, as said below
- up_scales: float32 [14336, 32], P(('seq', 'tensor')), may hold values from 0.00125 to 0.00625
- down_codes: bfloat16 [14336, 4096], P('seq', 'tensor'), may hold values from -8 to 7, as said below
- down_scales: float32 [112, 4096], P('seq', 'tensor'), may hold values from 0.0006681531 to 0.0033407656
Outputs:
- output: bfloat16 [4096, 4096], P(('dp', 'seq'), 'tensor'), parts along dimension 0
There are 4 independent parts, one for each index of `dp`. A program takes and returns all parts, laid end to end along the dimension named above; an argument that names none is the same for every part. Nothing has to cross between parts.
Inputs may be any that keep to these rules, and one draw needn't show every extreme that they name: `gate_codes`: whole numbers. `up_codes`: whole numbers. `down_codes`: whole numbers.
All inputs are finite; a program needn't handle non-finite values.
Results may differ from a plain program's by a relative error of at most 0.0076.
Values may be sent and summed in bfloat16 or wider, within the bound.
A program may use at most 64 MiB of HBM per device.

v0:
```python
import jax
import jax.numpy as jnp
import numpy as np
from jax import lax
from jax.sharding import PartitionSpec as P

WALSH = 512


def sylvester(table_order):
    result_table = jnp.ones((1, 1), jnp.float32)
    kernel_two = jnp.array([[1.0, 1.0], [1.0, -1.0]], jnp.float32)
    while result_table.shape[0] < table_order:
        result_table = jnp.kron(kernel_two, result_table)
    return result_table / jnp.sqrt(jnp.float32(table_order))


def paley_table():
    squares_mod = set((value * value % 13 for value in range(1, 13)))
    conference = np.zeros((14, 14))
    conference[0, 1:] = 1.0
    conference[1:, 0] = 1.0
    for row_pos in range(1, 14):
        for col_pos in range(1, 14):
            offset = (col_pos - row_pos) % 13
            if offset != 0:
                conference[row_pos, col_pos] = 1.0 if offset in squares_mod else -1.0
    kernel_first = np.array([[1.0, 1.0], [1.0, -1.0]])
    kernel_second = np.array([[1.0, -1.0], [-1.0, -1.0]])
    table = np.kron(conference, kernel_first) + np.kron(np.eye(14), kernel_second)
    return jnp.asarray(table / np.sqrt(28.0), jnp.float32)


def rotate(hidden):
    row_total = hidden.shape[0]
    precise = lax.Precision.HIGHEST
    values = hidden.astype(jnp.float32).reshape(row_total, 28, WALSH)
    values = jnp.einsum("ncp,pq->ncq", values, sylvester(WALSH), precision=precise)
    values = jnp.einsum("ncq,cb->nbq", values, paley_table(), precision=precise)
    return values.reshape(row_total, 28 * WALSH).astype(jnp.bfloat16)


def expand_rows(codes, scales):
    group_count = scales.shape[0]
    values = codes.astype(jnp.float32).reshape(
        group_count, codes.shape[0] // group_count, codes.shape[1]
    )
    values = values * scales[:, None, :]
    return values.reshape(codes.shape).astype(jnp.bfloat16)


def expand_cols(codes, scales):
    group_count = scales.shape[1]
    values = codes.astype(jnp.float32).reshape(
        codes.shape[0], group_count, codes.shape[1] // group_count
    )
    values = values * scales[:, :, None]
    return values.reshape(codes.shape).astype(jnp.bfloat16)


def swiglu_rows(products, unit_count):
    return (jax.nn.silu(products[:, :unit_count]) * products[:, unit_count:]).astype(jnp.bfloat16)


def local(tokens, gate_codes, gate_scales, up_codes, up_scales, down_codes, down_scales):
    w_gate = expand_cols(gate_codes, gate_scales)
    w_up = expand_cols(up_codes, up_scales)
    w_down = expand_rows(down_codes, down_scales)
    row_count = tokens.shape[0]
    unit_count = w_gate.shape[0]
    seq_count = lax.axis_size("seq")
    tensor_count = lax.axis_size("tensor")
    device_total = seq_count * tensor_count
    token_total = row_count * seq_count
    share_rows = row_count // tensor_count
    paired = jnp.concatenate([w_gate, w_up], axis=0)
    products = lax.dot_general(
        lax.all_gather(tokens, "seq", axis=0, tiled=True),
        paired,
        (((1,), (1,)), ((), ())),
        preferred_element_type=jnp.float32,
    )
    hidden = swiglu_rows(products, unit_count)
    outgoing = hidden.reshape(device_total, share_rows, unit_count)
    turned = rotate(
        lax.all_to_all(outgoing, ("seq", "tensor"), split_axis=0, concat_axis=2, tiled=True)[0]
    )[None]
    returned = lax.all_to_all(turned, ("seq", "tensor"), split_axis=2, concat_axis=0, tiled=True)
    placed = returned.reshape(token_total, 1, unit_count)
    columns = lax.all_gather(placed, "tensor", axis=1, tiled=True)
    columns = columns.reshape(token_total, tensor_count * unit_count)
    summed = lax.psum_scatter(
        jnp.dot(columns, w_down, preferred_element_type=jnp.float32),
        "seq",
        scatter_dimension=0,
        tiled=True,
    )
    return summed.astype(jnp.bfloat16)


def solution(mesh):
    return jax.shard_map(
        local,
        mesh=mesh,
        in_specs=(
            P(("dp", "seq"), None),
            P(("seq", "tensor"), None),
            P(("seq", "tensor"), None),
            P(("seq", "tensor"), None),
            P(("seq", "tensor"), None),
            P("seq", "tensor"),
            P("seq", "tensor"),
        ),
        out_specs=P(("dp", "seq"), "tensor"),
        check_vma=False,
    )
```

profile of v0, /device:TPU:1, one launch (start us, length us, event | category | flops | bytes accessed | tf_op | source)
XLA Modules:
  0.0 451.6 jit_solution(3405957555811572737)
XLA Ops:
  6.5 0.7 all-gather.3.cloned.1.call-update
  7.3 0.8 copy.18
  8.1 0.8 copy.19
  8.9 0.8 broadcast_multiply_fusion.6
  9.7 0.1 mul.284
  9.8 0.8 broadcast_multiply_fusion.5
  10.6 0.8 broadcast_multiply_fusion.4
  11.4 0.1 mul.290
  11.5 0.8 broadcast_multiply_fusion.3
  12.2 0.1 mul.293
  12.3 0.8 broadcast_multiply_fusion.2
  13.1 0.1 mul.296
  13.2 0.8 broadcast_multiply_fusion.1
  14.0 0.1 mul.299
  14.1 0.5 mul.266
  14.6 0.5 mul.269
  15.2 0.1 copy-done
  15.3 0.3 copy-done.1
  15.5 3.6 fusion
  19.1 108.9 %all-gather.3.cloned.1.call-done = bf16[1024,4096]{1,0:T(8,128)(2,1)} async-done(((bf16[64,4096]{1,0:T(8,128)(2,1)}), bf16[1024,4096]{1,0:T(8,128)(2,1)}) %all-gather.3.cloned.1.call-update) | async-done | bytes 8388624 | tf_op jit(solution)/shard_map/all_gather | solution.py:78
  128.0 6.0 %fusion.7 = f32[1024,224]{0,1:T(8,128)S(1)} fusion(bf16[1024,4096]{1,0:T(8,128)(2,1)} %all-gather.3.cloned.1.call-done, bf16[112,4096]{1,0:T(8,128)(2,1)S(1)} %get-tuple-element.5, bf16[112,4096]{1,0:T(8,128)(2,1)S(1)} %get-tuple-element.6), kind=kOutput, calls=%fused_computation.10 | convolution fusion | flops 1882718208 | bytes 11141120 | tf_op jit(solution)/shard_map/dot_general | solution.py:77
  134.0 0.1 fusion.11
  134.1 0.8 copy.20
  135.0 10.8 %all-to-all-start = ((bf16[128,8,112]{2,1,0:T(8,128)(2,1)}), bf16[128,8,112]{2,1,0:T(8,128)(2,1)S(1)}, u32[]{:S(2)}, u32[]{:S(2)}) async-start(bf16[128,8,112]{2,1,0:T(8,128)(2,1)} %bitcast.1), calls=%async_computation | async-start | bytes 524288 | tf_op jit(solution)/shard_map/all_to_all | solution.py:86
  145.7 0.2 all-gather.5.cloned.1.call-start
  146.0 0.1 broadcast_multiply_fusion
  146.2 0.5 multiply_multiply_fusion
  146.7 0.8 reshape.186
  147.5 14.2 %all-to-all-done = bf16[128,8,112]{2,1,0:T(8,128)(2,1)S(1)} async-done(((bf16[128,8,112]{2,1,0:T(8,128)(2,1)}), bf16[128,8,112]{2,1,0:T(8,128)(2,1)S(1)}, u32[]{:S(2)}, u32[]{:S(2)}) %all-to-all-start) | async-done | bytes 229408 | tf_op jit(solution)/shard_map/all_to_all | solution.py:86
  161.8 0.6 reshape.183
  162.4 0.7 fusion.13
  163.0 0.6 fusion.10
  163.6 0.1 convert_element_type.48
  163.8 11.5 %copy.22 = bf16[1,8,14336]{1,0,2:T(2,128)(2,1)} copy(bf16[1,8,14336]{2,1,0:T(8,128)(2,1)S(1)} %convert_element_type.48) | data formatting | bytes 458752 | tf_op jit(solution)/shard_map/convert_element_type | solution.py:40
  175.2 0.5 broadcast.56
  175.8 79.8 %reduce = bf16[14336,8]{1,0:T(8,128)(2,1)} reduce(bf16[14336,1,8]{2,1,0:T(2,128)(2,1)} %bitcast.44, bf16[]{:T(256)} %broadcast.56), dimensions={1}, to_apply=%bitcast.33.reduce_sub_computation | reduce | bytes 458754
  255.6 5.5 %reshape.189 = bf16[128,2,448]{2,1,0:T(2,128)(2,1)S(1)} reshape(bf16[14336,8]{1,0:T(8,128)(2,1)} %reduce) | data formatting | bytes 458752
  261.1 23.4 %all_to_all.30 = bf16[128,2,448]{2,1,0:T(2,128)(2,1)S(1)} all-to-all(bf16[128,2,448]{2,1,0:T(2,128)(2,1)S(1)} %reshape.189), channel_id=1, replica_groups=mesh['dp'=4,'seq'=16,'tensor'=8] {'seq','tensor'}, dimensions={0} | all-to-all | bytes 458752 | tf_op jit(solution)/shard_map/all_to_all | solution.py:88
  284.5 9.0 %reshape.190 = bf16[14336,1,8]{2,1,0:T(2,128)(2,1)} reshape(bf16[128,2,448]{2,1,0:T(2,128)(2,1)S(1)} %all_to_all.30) | data formatting | bytes 458752
  293.5 13.4 %copy.23 = bf16[1,8,14336]{2,1,0:T(8,128)(2,1)S(1)} copy(bf16[1,8,14336]{1,0,2:T(2,128)(2,1)} %bitcast.45) | data formatting | bytes 458752 | tf_op jit(solution)/shard_map/all_to_all | solution.py:88
  306.9 0.4 all_to_all.26
  307.3 0.2 copy.34
  307.5 0.8 copy.25
  308.4 0.2 fusion.6
  308.6 33.9 %all-gather.5.cloned.1.call-done = bf16[1024,8,112]{0,2,1:T(8,128)(2,1)} async-done(((bf16[1024,1,112]{0,2,1:T(8,128)(2,1)}), bf16[1024,8,112]{0,2,1:T(8,128)(2,1)}) %all-gather.5.cloned.1.call-update) | async-done | bytes 1835024 | tf_op jit(solution)/shard_map/all_gather | solution.py:90
  342.5 4.1 fusion.14
  346.6 96.9 %reduce-scatter.2.cloned.1.call-done = f32[64,512]{1,0:T(8,128)} async-done(((f32[1024,512]{1,0:T(8,128)}), f32[64,512]{1,0:T(8,128)}) %reduce-scatter.2.cloned.1.call-update) | async-done | bytes 131088 | tf_op jit(solution)/shard_map/reduce_scatter | solution.py:92
  443.5 1.5 convert_element_type.51
  (17 shorter events, 0.2 us)
Async XLA Ops:
  6.5 121.4 %all-gather.3.cloned.1.call-start = ((), (), s32[]{:S(2)}) async-start(), calls=%async_computation.3 | async-start | bytes 8912896 | tf_op jit(solution)/shard_map/all_gather | solution.py:78
  14.1 1.2 copy-start
  14.1 1.5 copy-start.1
  134.0 12.0 %copy-start.3 = (f32[2,2]{1,0:T(2,128)S(1)}, f32[2,2]{1,0:T(2,128)}, u32[]{:S(2)}) copy-start(f32[2,2]{1,0:T(2,128)} %constant.12.clone) | copy-start | bytes 52
  135.0 26.8 %all-to-all-start = ((bf16[128,8,112]{2,1,0:T(8,128)(2,1)}), bf16[128,8,112]{2,1,0:T(8,128)(2,1)S(1)}, u32[]{:S(2)}, u32[]{:S(2)}) async-start(bf16[128,8,112]{2,1,0:T(8,128)(2,1)} %bitcast.1), calls=%async_computation | async-start | bytes 524288 | tf_op jit(solution)/shard_map/all_to_all | solution.py:86
  145.7 196.7 %all-gather.5.cloned.1.call-start = ((), (), s32[]{:S(2)}) async-start(), calls=%async_computation.4 | async-start | bytes 2064384 | tf_op jit(solution)/shard_map/all_gather | solution.py:90
  147.5 15.5 %copy-start.5 = (f32[28,28,1]{0,1,2:T(8,128)S(1)}, f32[28,28,1]{0,1,2:T(8,128)}, u32[]{:S(2)}) copy-start(f32[28,28,1]{0,1,2:T(8,128)} %constant.19) | copy-start | bytes 9412
  293.5 14.9 %copy-start.4 = (f32[7,512]{1,0:T(8,128)S(1)}, f32[7,512]{1,0:T(8,128)}, u32[]{:S(2)}) copy-start(f32[7,512]{1,0:T(8,128)} %param.15) | copy-start | bytes 43012
  306.9 1.5 copy-start.2
  308.4 135.1 %reduce-scatter.2.cloned.1.call-start = ((), (), s32[]{:S(2)}) async-start(), calls=%async_computation.5 | async-start | bytes 2228224 | tf_op jit(solution)/shard_map/reduce_scatter | solution.py:92
Sparse Core Ops, SparseCore 0:
  10.6 117.2 all-gather.2
  308.5 33.9 all-gather.4
  347.3 96.1 reduce-scatter.1
where the time goes:
time: 452 us
  waiting for transfers between devices  255 us (56%)
  other arithmetic  90.5 us (20%)
  local copies, waits for them, and re-layouts  47.4 us (10%)
  blocking collectives  23.4 us (5%)
  between operations  13.3 us (3%)
  matrix products  11.4 us (3%)
  starting transfers between devices  11 us (2%)
    all_gather x1, waiting for transfers between devices, local(): lax.all_gather(tokens, 'seq', axis=0, tiled=True)  109 us
    reduce_scatter x1, waiting for transfers between devices, local(): lax.psum_scatter(jnp.dot(columns, w_down, preferred_element_type=jnp.floa...  96.9 us
    unnamed x1, other arithmetic  79.8 us
    all_gather x1, waiting for transfers between devices, local(): columns = lax.all_gather(placed, 'tensor', axis=1, tiled=True)  33.9 us
    all_to_all x1, blocking collectives, local(): lax.all_to_all(turned, ('seq', 'tensor'), split_axis=2, concat_axis=0, ti...  23.4 us
    unnamed x18, local copies, waits for them, and re-layouts  17.1 us
    all_to_all x1, waiting for transfers between devices, local(): lax.all_to_all(outgoing, ('seq', 'tensor'), split_axis=0, concat_axis=2,...  14.2 us
    all_to_all x3, local copies, waits for them, and re-layouts, local(): lax.all_to_all(turned, ('seq', 'tensor'), split_axis=2, concat_axis=0, ti...  13.9 us
  transfers between devices with their start and end apart: 4, of which 4 were waited for; matrix products, arithmetic and copies ran while one was open for 3% of the time, Pallas kernels for 0%

commit v1 on v0

v1 whole, which is shorter than its diff:
```python
import functools

import jax
import jax.numpy as jnp
import numpy as np
from jax import lax
from jax.experimental import pallas as pl
from jax.experimental.pallas import tpu as pltpu
from jax.sharding import PartitionSpec as P

MESH = pl.DeviceIdType.MESH
WALSH = 512
CHUNKS = 7
SKEW = 2
NORM = 1.0 / np.sqrt(28.0 * 512.0)
NT = (((1,), (1,)), ((), ()))


def sylvester_signs(order):
    table = np.ones((1, 1), np.float32)
    while table.shape[0] < order:
        table = np.kron(np.array([[1.0, 1.0], [1.0, -1.0]], np.float32), table)
    return table


def paley_signs():
    squares = {value * value % 13 for value in range(1, 13)}
    conference = np.zeros((14, 14))
    conference[0, 1:] = 1.0
    conference[1:, 0] = 1.0
    for row in range(1, 14):
        for col in range(1, 14):
            offset = (col - row) % 13
            if offset != 0:
                conference[row, col] = 1.0 if offset in squares else -1.0
    first = np.array([[1.0, 1.0], [1.0, -1.0]])
    second = np.array([[1.0, -1.0], [-1.0, -1.0]])
    return (np.kron(conference, first) + np.kron(np.eye(14), second)).astype(np.float32)


def row_of(core, chunk):
    return pl.multiple_of(jnp.where(chunk < 4, core * 64 + chunk * 16, 128 + core * 48 + (chunk - 4) * 16), 16)


def kernel(
    tokens_in, gate_in, gate_scale_in, up_in, up_scale_in, down_in, down_scale_in, signs_in, paley,
    out_ref,
    tok, codes, scales, dcodes, dscales, signs, weights, turned, pieces, gathered, mixed, hidden, final, partial, sums,
    load_sem, tok_s, tok_r, chain_s, chain_r, own_s, own_r, share_s, share_r, piece_s, piece_r, gath_s, gath_r,
    ring_s, ring_r, ringc_s, ringc_r, own_piece_s, own_piece_r, hid_s, hid_r, sum_s, sum_r,
):
    d, s, z = lax.axis_index("dp"), lax.axis_index("seq"), lax.axis_index("tensor")
    x, yh, c = s // 4, (s // 2) % 2, s % 2
    y = yh * 4 + d

    def at_y(row, core):
        return (row % 4, x * 4 + (row // 4) * 2 + core, z)

    sib = (d, s + 1 - 2 * c, z)
    x_peers = [(d, (s + 4 * k) % 16, z) for k in (1, 3, 2)]
    z_peers = [(d, s, (z + k) % 8) for k in range(1, 8)]
    y_up, y_down = at_y((y + 1) % 8, c), at_y((y + 7) % 8, c)
    y_opp = (y + 4) % 8
    opp, opp_sib = at_y(y_opp, c), at_y(y_opp, 1 - c)

    def remote(src, dst, ss, rs, dev):
        return pltpu.make_async_remote_copy(
            src_ref=src, dst_ref=dst, send_sem=ss, recv_sem=rs, device_id=dev, device_id_type=MESH
        )

    loads = [
        pltpu.make_async_copy(src, dst, load_sem.at[i])
        for i, (src, dst) in enumerate(
            [
                (tokens_in, tok.at[0]), (gate_in, codes.at[0]), (up_in, codes.at[1]), (gate_scale_in, scales.at[0]),
                (up_scale_in, scales.at[1]), (down_in, dcodes), (down_scale_in, dscales), (signs_in, signs),
            ]
        )
    ]
    for load in loads:
        load.start()
    barrier = pltpu.get_barrier_semaphore()
    peers = [sib, *x_peers, *z_peers, y_up, y_down, opp, opp_sib]
    for peer in peers:
        pl.semaphore_signal(barrier, inc=1, device_id=peer, device_id_type=MESH)
    pl.semaphore_wait(barrier, len(peers))

    loads[0].wait()
    tok_copies = [
        remote(tok.at[0], tok.at[slot], tok_s.at[i], tok_r.at[i], x_peers[i]) for i, slot in enumerate((2, 1, 3))
    ]
    for copy in tok_copies:
        copy.start()

    for load in loads[1:5]:
        load.wait()

    def chain(kind, chunk):
        last = (d == 3) if kind == 0 else (d == 0)
        half = jnp.where(last, 0, 1)
        rows = pl.ds(row_of(c, chunk), 16)
        return remote(
            weights.at[kind, half, rows, :], weights.at[kind, 1, rows, :],
            chain_s.at[kind, chunk], chain_r.at[kind, chunk], y_up if kind == 0 else y_down,
        )

    def own(kind, chunk):
        rows = pl.ds(row_of(c, chunk), 16)
        return remote(
            weights.at[kind, 0, rows, :], weights.at[kind, 0, rows, :],
            own_s.at[kind, chunk], own_r.at[kind, chunk], sib,
        )

    def share(kind, chunk):
        rows = pl.ds(row_of(c, chunk), 16)
        return remote(
            weights.at[kind, 1, rows, :], weights.at[kind, 1, rows, :],
            share_s.at[kind, chunk], share_r.at[kind, chunk], sib,
        )

    def expand(chunk, _):
        at = pl.multiple_of(chunk * 16, 16)
        row = row_of(c, chunk)
        for kind in range(2):
            scale = scales[kind, pl.ds(at, 16), :]
            for group in range(32):
                lanes = slice(group * 128, group * 128 + 128)
                value = codes[kind, pl.ds(at, 16), lanes].astype(jnp.float32) * scale[:, group : group + 1]
                weights[kind, 0, pl.ds(row, 16), lanes] = value.astype(jnp.bfloat16)

            @pl.when(d == (3 if kind == 0 else 0))
            def _():
                chain(kind, chunk).start()

            own(kind, chunk).start()
        return 0

    lax.fori_loop(0, CHUNKS, expand, 0)

    for load in loads[5:]:
        load.wait()
    for group in range(7):
        rows = slice(group * 128, group * 128 + 128)
        value = dcodes[rows, :].astype(jnp.float32) * dscales[group : group + 1, :]
        turned[:, rows] = value.astype(jnp.bfloat16).astype(jnp.float32).T.astype(jnp.bfloat16)

    own_lanes = pl.ds(pl.multiple_of((yh * 2 + c) * 896, 128), 896)

    def rows_for(row, core):
        return pl.ds(pl.multiple_of(row * 64 + core * 32, 32), 32)

    piece_copies = [
        remote(turned.at[rows, :], pieces.at[0, :, own_lanes], piece_s.at[i], piece_r.at[i], peer)
        for i, (rows, peer) in enumerate(
            [(rows_for(y, 1 - c), sib), (rows_for(y_opp, c), opp), (rows_for(y_opp, 1 - c), opp_sib)]
        )
    ]
    for copy in piece_copies:
        copy.start()
    pieces[0, :, own_lanes] = turned[rows_for(y, c), :]

    def steps(first, end):
        def body(n, _):
            for kind in range(2):
                hops = d if kind == 0 else 3 - d
                chunk = n - SKEW * hops

                @pl.when(jnp.logical_and(chunk >= 0, chunk < CHUNKS))
                def _():
                    chain(kind, chunk).wait_recv()

                    @pl.when(hops < 3)
                    def _():
                        chain(kind, chunk).start()

                    share(kind, chunk).start()

            return 0

        lax.fori_loop(first, end, body, 0)

    def wait_own(first, end):
        def body(chunk, _):
            for kind in range(2):
                own(kind, chunk).wait_recv()
            return 0

        lax.fori_loop(first, end, body, 0)

    def wait_share(first, end):
        def body(chunk, _):
            for kind in range(2):
                share(kind, chunk).wait_recv()
            return 0

        lax.fori_loop(first, end, body, 0)

    def units(half, rows, lane_tokens):
        gate = lax.dot_general(weights[0, half, rows, :], lane_tokens, NT, preferred_element_type=jnp.float32)
        up = lax.dot_general(weights[1, half, rows, :], lane_tokens, NT, preferred_element_type=jnp.float32)
        return (gate / (1.0 + jnp.exp(-gate)) * up).astype(jnp.bfloat16)

    def place(group, half, core, first, value):
        a = jnp.where(half == 0, yh, 1 - yh) * 2 + core
        rows = pl.ds(pl.multiple_of(z * 112 + first, 16), value.shape[0])
        hidden[group, a, rows, :] = value

    def spread(index, groups, half, first, count):
        pair = pl.ds(jnp.where(half == 0, yh, 1 - yh) * 2, 2)
        rows = pl.ds(pl.multiple_of(z * 112 + first, 16), count)
        block = hidden.at[groups, pair, rows, :]
        return [remote(block, block, hid_s.at[index, k], hid_r.at[index, k], z_peers[k]) for k in range(7)]

    def own_units(group):
        result = units(0, slice(0, 224), tok[2 * group : 2 * group + 2].reshape(128, 4096))
        for core in range(2):
            place(group, 0, core, 0, result[core * 64 : core * 64 + 64])
            place(group, 0, core, 64, result[128 + core * 48 : 176 + core * 48])
        copies = spread(group, pl.ds(group, 1), 0, 0, 112)
        for copy in copies:
            copy.start()
        return copies

    def other_units(index, first, count):
        result = units(1, slice(first * 2, first * 2 + count * 2), tok[...].reshape(256, 4096))
        for group in range(2):
            for core in range(2):
                place(group, 1, core, first, result[core * count : core * count + count, group * 128 : group * 128 + 128])
        copies = spread(index, pl.ds(0, 2), 1, first, count)
        for copy in copies:
            copy.start()
        return copies

    waits = list(piece_copies) + list(tok_copies)

    steps(0, 1)
    for copy in piece_copies:
        copy.wait_recv()
    gath_copies = [
        remote(pieces.at[0], pieces.at[slot], gath_s.at[i], gath_r.at[i], x_peers[i]) for i, slot in enumerate((2, 1, 3))
    ]
    for copy in gath_copies:
        copy.start()
    waits += gath_copies
    steps(1, 4)

    wait_own(0, CHUNKS)
    tok_copies[1].wait_recv()
    hid_copies = own_units(0)

    steps(4, 6)
    for copy in gath_copies:
        copy.wait_recv()
    for part in range(4):
        sums_of = [None] * 7
        for slot, offset in enumerate((0, 1, 3, 2)):
            for block in range(7):
                lanes = slice(block * 512 + part * 128, block * 512 + part * 128 + 128)
                value = pieces[slot, :, lanes].astype(jnp.float32)
                for i in range(7):
                    term = value * paley[((x + offset) % 4) * 7 + block, x * 7 + i]
                    sums_of[i] = term if sums_of[i] is None else sums_of[i] + term
        for i in range(7):
            mixed[i * 32 : i * 32 + 32, part * 128 : part * 128 + 128] = sums_of[i]
    high = mixed[...].astype(jnp.bfloat16)
    low = (mixed[...] - high.astype(jnp.float32)).astype(jnp.bfloat16)
    table = signs[...]
    rotated = jnp.dot(high, table, preferred_element_type=jnp.float32)
    rotated = (rotated + jnp.dot(low, table, preferred_element_type=jnp.float32)) * NORM
    my_rows = rows_for(y, c)
    for i in range(7):
        final[my_rows, i * 512 : i * 512 + 512] = rotated[i * 32 : i * 32 + 32].astype(jnp.bfloat16)

    def ring(way, step, half):
        row = (y + 8 - step) % 8 if way == 0 else (y + step) % 8
        block = final.at[rows_for(row, c), pl.ds(half * 1792, 1792)]
        return remote(
            block, block, ring_s.at[way, step, half], ring_r.at[way, step, half], y_up if way == 0 else y_down
        )

    def ring_core(way, step, half):
        row = (y + 7 - step) % 8 if way == 0 else (y + 1 + step) % 8
        block = final.at[rows_for(row, c), pl.ds(half * 1792, 1792)]
        return remote(block, block, ringc_s.at[way, step, half], ringc_r.at[way, step, half], sib)

    def halves(way, step):
        return (0, 1) if step < 3 else (way,)

    own_piece = remote(
        final.at[my_rows, :], final.at[my_rows, :], own_piece_s.at[0], own_piece_r.at[0], sib
    )
    for half in range(2):
        for way in range(2):
            ring(way, 0, half).start()
    own_piece.start()

    def ring_step(step):
        for half in range(2):
            for way in range(2):
                if half in halves(way, step):
                    ring(way, step, half).wait_recv()
                    if step < 3 and half in halves(way, step + 1):
                        ring(way, step + 1, half).start()
                    ring_core(way, step, half).start()

    steps(6, 8)
    tok_copies[0].wait_recv()
    tok_copies[2].wait_recv()
    hid_copies += own_units(1)
    steps(8, 10)
    wait_share(0, 4)
    hid_copies += other_units(2, 0, 64)
    ring_step(0)
    steps(10, CHUNKS + 3 * SKEW)
    wait_share(4, CHUNKS)
    hid_copies += other_units(3, 64, 48)
    for step in range(1, 4):
        ring_step(step)

    for copy in hid_copies:
        copy.wait_recv()
    own_piece.wait_recv()
    for step in range(4):
        for way in range(2):
            for half in halves(way, step):
                ring_core(way, step, half).wait_recv()

    for group in range(2):
        block = hidden[group].reshape(3584, 128)
        result = jnp.dot(final[...], block, preferred_element_type=jnp.float32).T
        partial[group * 128 : group * 128 + 128, :] = result.astype(jnp.bfloat16)
        if group == 0:
            total = result[:64]
    sum_copies = [
        remote(partial.at[pl.ds(64 * (i + 1), 64), :], sums.at[i], sum_s.at[i], sum_r.at[i], x_peers[i]) for i in range(3)
    ]
    for copy in sum_copies:
        copy.start()
    for copy in sum_copies:
        copy.wait_recv()
    for i in range(3):
        total = total + sums[i].astype(jnp.float32)
    out_ref[...] = total.astype(jnp.bfloat16)

    for copy in waits + hid_copies + sum_copies + [own_piece]:
        copy.wait_send()

    def end(chunk, _):
        for kind in range(2):
            chain(kind, chunk).wait_send()
            own(kind, chunk).wait_send()
            share(kind, chunk).wait_send()
        return 0

    lax.fori_loop(0, CHUNKS, end, 0)
    for step in range(4):
        for way in range(2):
            for half in halves(way, step):
                ring(way, step, half).wait_send()
                ring_core(way, step, half).wait_send()


def local(tokens, gate_codes, gate_scales, up_codes, up_scales, down_codes, down_scales):
    dma = pltpu.SemaphoreType.DMA
    bf16, f32 = jnp.bfloat16, jnp.float32
    anywhere = pl.BlockSpec(memory_space=pl.ANY)
    signs = jnp.asarray(sylvester_signs(WALSH), bf16)
    paley = jnp.asarray(paley_signs())
    return pl.pallas_call(
        kernel,
        out_shape=jax.ShapeDtypeStruct((64, 512), bf16),
        in_specs=[anywhere] * 8 + [pl.BlockSpec(memory_space=pltpu.SMEM)],
        out_specs=pl.BlockSpec(memory_space=pltpu.VMEM),
        scratch_shapes=[
            pltpu.VMEM((4, 64, 4096), bf16),
            pltpu.VMEM((2, 112, 4096), bf16),
            pltpu.VMEM((2, 112, 32), f32),
            pltpu.VMEM((896, 512), bf16),
            pltpu.VMEM((7, 512), f32),
            pltpu.VMEM((512, 512), bf16),
            pltpu.VMEM((2, 2, 224, 4096), bf16),
            pltpu.VMEM((512, 896), bf16),
            pltpu.VMEM((4, 32, 3584), bf16),
            pltpu.VMEM((8, 128), f32),
            pltpu.VMEM((224, 512), f32),
            pltpu.VMEM((2, 4, 896, 128), bf16),
            pltpu.VMEM((512, 3584), bf16),
            pltpu.VMEM((256, 512), bf16),
            pltpu.VMEM((3, 64, 512), bf16),
            dma((8,)),
            dma((3,)), dma((3,)),
            dma((2, CHUNKS)), dma((2, CHUNKS)),
            dma((2, CHUNKS)), dma((2, CHUNKS)),
            dma((2, CHUNKS)), dma((2, CHUNKS)),
            dma((3,)), dma((3,)),
            dma((3,)), dma((3,)),
            dma((2, 4, 2)), dma((2, 4, 2)),
            dma((2, 4, 2)), dma((2, 4, 2)),
            dma((1,)), dma((1,)),
            dma((4, 7)), dma((4, 7)),
            dma((3,)), dma((3,)),
        ],
        compiler_params=pltpu.CompilerParams(
            collective_id=0, has_side_effects=True, vmem_limit_bytes=56 * 1024 * 1024
        ),
        cost_estimate=pl.CostEstimate(flops=4 * 10**9, bytes_accessed=4 * 10**6, transcendentals=10**5),
        name="feed_forward",
    )(tokens, gate_codes, gate_scales, up_codes, up_scales, down_codes, down_scales, signs, paley)


def solution(mesh):
    return jax.shard_map(
        local,
        mesh=mesh,
        in_specs=(
            P(("dp", "seq"), None),
            P(("seq", "tensor"), None),
            P(("seq", "tensor"), None),
            P(("seq", "tensor"), None),
            P(("seq", "tensor"), None),
            P("seq", "tensor"),
            P("seq", "tensor"),
        ),
        out_specs=P(("dp", "seq"), "tensor"),
        check_vma=False,
    )
```

time: 452 us -> 106 us (0.23)
  waiting for transfers between devices: 255 us -> 0 us
  Pallas kernels: 0 us -> 102 us
  other arithmetic: 90.5 us -> 0 us
  local copies, waits for them, and re-layouts: 47.4 us -> 3.64 us
  blocking collectives: 23.4 us -> 0 us
  between operations: 13.3 us -> 0.01 us
  matrix products: 11.4 us -> 0 us
  starting transfers between devices: 11 us -> 0 us
    all_gather x2 -> x0, waiting for transfers between devices: 143 us -> none  [the longest x1 109 us: local(): lax.all_gather(tokens, 'seq', axis=0, tiled=True)]
    pallas_call x0 -> x1, Pallas kernels: none -> 102 us  [local(): pl.pallas_call(kernel, out_shape=jax.ShapeDtypeStruct((64, 512), bf16), i...]
    reduce_scatter x1 -> x0, waiting for transfers between devices: 96.9 us -> none  [local(): lax.psum_scatter(jnp.dot(columns, w_down, preferred_element_type=jnp.floa...]
    unnamed x1 -> x0, other arithmetic: 79.8 us -> none
    all_to_all x1 -> x0, blocking collectives: 23.4 us -> none  [local(): lax.all_to_all(turned, ('seq', 'tensor'), split_axis=2, concat_axis=0, ti...]
    all_to_all x1 -> x0, waiting for transfers between devices: 14.2 us -> none  [local(): lax.all_to_all(outgoing, ('seq', 'tensor'), split_axis=0, concat_axis=2,...]
    all_to_all x4 -> x0, local copies, waits for them, and re-layouts: 14 us -> none  [the longest x3 13.9 us: local(): lax.all_to_all(turned, ('seq', 'tensor'), split_axis=2, concat_axis=0, ti...]
    unnamed x18 -> x5, local copies, waits for them, and re-layouts: 17.1 us -> 3.64 us
  transfers between devices with their start and end apart: 4 -> 0, of which waited for: 4 -> 0; matrix products, arithmetic and copies ran while one was open for 3% -> 0% of each run, Pallas kernels for 0% -> 0%
where the time goes in v1:
time: 106 us; the launch traced here: 105 us
  Pallas kernels  102 us (96%)
  local copies, waits for them, and re-layouts  3.64 us (3%)
    pallas_call x1, Pallas kernels, local(): pl.pallas_call(kernel, out_shape=jax.ShapeDtypeStruct((64, 512), bf16), i...  102 us
    unnamed x5, local copies, waits for them, and re-layouts  3.64 us

profile of v1, /device:TPU:1, one launch (start us, length us, event | category | flops | bytes accessed | tf_op | source)
XLA Modules:
  0.0 105.3 jit_solution(1400035680968667638)
XLA Ops:
  0.0 0.0 copy-start
  0.0 1.4 %copy.10.gate_scale_in = f32[112,32]{1,0:T(8,128)} copy(f32[112,32]{0,1:T(8,128)} %param.11) | data formatting | bytes 28672 | tf_op args[2]
  1.5 0.0 copy-done
  1.5 0.7 copy.11.up_scale_in
  2.2 101.6 %feed_forward.1 = bf16[64,512]{1,0:T(8,128)(2,1)} custom-call(bf16[64,4096]{1,0:T(8,128)(2,1)} %tokens_in.1, bf16[112,4096]{1,0:T(8,128)(2,1)} %gate_in.1, f32[112,32]{1,0:T(8,128)} %copy.10.gate_scale_in, bf16[112,4096]{1,0:T(8,128)(2,1)} %up_in.1, f32[112,32]{1,0:T(8,128)} %copy.11.up_scale_in, bf16[896,512]{1,0:T(8,128)(2,1)} %down_in.1, ...), custom_call_target="tpu_custom_call" | custom-call | flops 4000000000 | bytes 4000000 | tf_op jit(solution)/shard_map/feed_forward/pallas_call | solution.py:369
  103.8 1.5 %copy.13 = bf16[64,512]{1,0:T(8,128)(2,1)} copy(bf16[64,512]{1,0:T(8,128)(2,1)} %feed_forward.1) | data formatting | bytes 131072
Async XLA Ops:
  0.0 1.5 %copy-start = (f32[112,32]{0,1:T(8,128)S(1)}, f32[112,32]{0,1:T(8,128)}, u32[]{:S(2)}) copy-start(f32[112,32]{0,1:T(8,128)} %param.13) | copy-start | bytes 43012

commit v2 on v1

v2 whole, which is shorter than its diff:
```python
import functools

import jax
import jax.numpy as jnp
import numpy as np
from jax import lax
from jax.experimental import pallas as pl
from jax.experimental.pallas import tpu as pltpu
from jax.sharding import PartitionSpec as P

MESH = pl.DeviceIdType.MESH
WALSH = 512
CHUNKS = 7
PARTS = 2
WIDTH = 4096 // PARTS
SKEW = 3
STEPS = CHUNKS * PARTS + 3 * SKEW
GROUPS = ((0, 32), (32, 32), (64, 32), (96, 16))
NORM = 1.0 / np.sqrt(28.0 * 512.0)
NT = (((1,), (1,)), ((), ()))


def sylvester_signs(order):
    table = np.ones((1, 1), np.float32)
    while table.shape[0] < order:
        table = np.kron(np.array([[1.0, 1.0], [1.0, -1.0]], np.float32), table)
    return table


def paley_signs():
    squares = {value * value % 13 for value in range(1, 13)}
    conference = np.zeros((14, 14))
    conference[0, 1:] = 1.0
    conference[1:, 0] = 1.0
    for row in range(1, 14):
        for col in range(1, 14):
            offset = (col - row) % 13
            if offset != 0:
                conference[row, col] = 1.0 if offset in squares else -1.0
    first = np.array([[1.0, 1.0], [1.0, -1.0]])
    second = np.array([[1.0, -1.0], [-1.0, -1.0]])
    return (np.kron(conference, first) + np.kron(np.eye(14), second)).astype(np.float32)


def row_of(core, chunk):
    return pl.multiple_of(jnp.where(chunk < 6, chunk // 2 * 64 + core * 32 + chunk % 2 * 16, 192 + core * 16), 16)


def kernel(
    tokens_in, gate_in, gate_scale_in, up_in, up_scale_in, down_in, down_scale_in, signs_in, paley,
    out_ref,
    tok, codes, scales, dcodes, dscales, signs, weights, turned, turned_scales, pieces, mixed, hidden, final, early, partial, sums,
    load_sem, tok_s, tok_r, tokf_s, tokf_r, chain_s, chain_r, own_s, own_r, share_s, share_r, piece_s, piece_r, gath_s, gath_r, gathf_s, gathf_r,
    ring_s, ring_r, ringc_s, ringc_r, own_piece_s, own_piece_r, hid_s, hid_r, sum_s, sum_r,
):
    d, s, z = lax.axis_index("dp"), lax.axis_index("seq"), lax.axis_index("tensor")
    x, yh, c = s // 4, (s // 2) % 2, s % 2
    y = yh * 4 + d

    def at_y(row, core):
        return (row % 4, x * 4 + (row // 4) * 2 + core, z)

    sib = (d, s + 1 - 2 * c, z)
    x_peers = [(d, (s + 4 * k) % 16, z) for k in (1, 3, 2)]
    z_peers = [(d, s, (z + k) % 8) for k in range(1, 8)]
    y_up, y_down = at_y((y + 1) % 8, c), at_y((y + 7) % 8, c)
    y_opp = (y + 4) % 8
    opp, opp_sib = at_y(y_opp, c), at_y(y_opp, 1 - c)

    def remote(src, dst, ss, rs, dev):
        return pltpu.make_async_remote_copy(
            src_ref=src, dst_ref=dst, send_sem=ss, recv_sem=rs, device_id=dev, device_id_type=MESH
        )

    loads = [
        pltpu.make_async_copy(src, dst, load_sem.at[i])
        for i, (src, dst) in enumerate(
            [
                (tokens_in, tok.at[0]), (gate_in, codes.at[0]), (up_in, codes.at[1]), (gate_scale_in, scales.at[0]),
                (up_scale_in, scales.at[1]), (down_in, dcodes), (down_scale_in, dscales), (signs_in, signs),
            ]
        )
    ]
    for load in loads:
        load.start()
    barrier = pltpu.get_barrier_semaphore()
    peers = [sib, *x_peers, *z_peers, y_up, y_down, opp, opp_sib]
    for peer in peers:
        pl.semaphore_signal(barrier, inc=1, device_id=peer, device_id_type=MESH)
    pl.semaphore_wait(barrier, len(peers))

    x_up, x_down, x_far = x_peers

    def tok_copy(way, half):
        rows = pl.ds(half * 32, 32)
        return remote(
            tok.at[0, rows], tok.at[2 - way, rows], tok_s.at[way, half], tok_r.at[way, half], (x_up, x_down)[way]
        )

    def tok_forward(way):
        rows = pl.ds(way * 32, 32)
        return remote(tok.at[2 - way, rows], tok.at[3, rows], tokf_s.at[way], tokf_r.at[way], (x_up, x_down)[way])

    def gath_copy(way, half):
        rows = pl.ds(half * 16, 16)
        return remote(
            pieces.at[0, rows], pieces.at[2 - way, rows], gath_s.at[way, half], gath_r.at[way, half],
            (x_up, x_down)[way],
        )

    def gath_forward(way):
        rows = pl.ds(way * 16, 16)
        return remote(
            pieces.at[2 - way, rows], pieces.at[3, rows], gathf_s.at[way], gathf_r.at[way], (x_up, x_down)[way]
        )

    loads[0].wait()
    for order in range(2):
        for way in range(2):
            tok_copy(way, way if order == 0 else 1 - way).start()

    for load in loads[5:]:
        load.wait()
    for group in range(7):
        rows = slice(group * 128, group * 128 + 128)
        value = dcodes[rows, :].astype(jnp.float32) * dscales[group : group + 1, :]
        turned[:, rows] = value.astype(jnp.bfloat16).astype(jnp.float32).T.astype(jnp.bfloat16)

    own_lanes = pl.ds(pl.multiple_of((yh * 2 + c) * 896, 128), 896)

    def rows_for(row, core):
        return pl.ds(pl.multiple_of(row * 64 + core * 32, 32), 32)

    piece_copies = [
        remote(turned.at[rows, :], pieces.at[0, :, own_lanes], piece_s.at[i], piece_r.at[i], peer)
        for i, (rows, peer) in enumerate(
            [(rows_for(y, 1 - c), sib), (rows_for(y_opp, c), opp), (rows_for(y_opp, 1 - c), opp_sib)]
        )
    ]
    for copy in piece_copies:
        copy.start()
    pieces[0, :, own_lanes] = turned[rows_for(y, c), :]

    for load in loads[1:5]:
        load.wait()

    def chain(kind, index):
        last = (d == 3) if kind == 0 else (d == 0)
        half = jnp.where(last, 0, 1)
        rows = pl.ds(row_of(c, index // PARTS), 16)
        lanes = pl.ds(pl.multiple_of(index % PARTS * WIDTH, WIDTH), WIDTH)
        return remote(
            weights.at[kind, half, rows, lanes], weights.at[kind, 1, rows, lanes],
            chain_s.at[kind, index], chain_r.at[kind, index], y_up if kind == 0 else y_down,
        )

    def own(kind, chunk):
        rows = pl.ds(row_of(c, chunk), 16)
        return remote(
            weights.at[kind, 0, rows, :], weights.at[kind, 0, rows, :],
            own_s.at[kind, chunk], own_r.at[kind, chunk], sib,
        )

    def share(kind, index):
        rows = pl.ds(row_of(c, index // PARTS), 16)
        lanes = pl.ds(pl.multiple_of(index % PARTS * WIDTH, WIDTH), WIDTH)
        block = weights.at[kind, 1, rows, lanes]
        return remote(block, block, share_s.at[kind, index], share_r.at[kind, index], sib)

    for kind in range(2):
        turned_scales[kind] = scales[kind].T

    def expand(chunk, _):
        at = pl.multiple_of(chunk * 16, 16)
        row = row_of(c, chunk)
        for kind in range(2):
            scale = turned_scales[kind, pl.ds(at, 16), :]
            for group in range(32):
                lanes = slice(group * 128, group * 128 + 128)
                value = codes[kind, pl.ds(at, 16), lanes].astype(jnp.float32) * scale[:, group : group + 1]
                weights[kind, 0, pl.ds(row, 16), lanes] = value.astype(jnp.bfloat16)

            @pl.when(d == (3 if kind == 0 else 0))
            def _():
                for part in range(PARTS):
                    chain(kind, chunk * PARTS + part).start()

            own(kind, chunk).start()
        return 0

    lax.fori_loop(0, CHUNKS, expand, 0)

    def steps(first, end):
        def body(n, _):
            for kind in range(2):
                hops = d if kind == 0 else 3 - d
                index = n - SKEW * hops

                @pl.when(jnp.logical_and(index >= 0, index < CHUNKS * PARTS))
                def _():
                    chain(kind, index).wait_recv()

                    @pl.when(hops < 3)
                    def _():
                        chain(kind, index).start()

                    share(kind, index).start()

            return 0

        lax.fori_loop(first, end, body, 0)

    def wait_each(copy, first, end):
        def body(index, _):
            for kind in range(2):
                copy(kind, index).wait_recv()
            return 0

        lax.fori_loop(first, end, body, 0)

    def units(half, rows, lane_tokens):
        gate = lax.dot_general(weights[0, half, rows, :], lane_tokens, NT, preferred_element_type=jnp.float32)
        up = lax.dot_general(weights[1, half, rows, :], lane_tokens, NT, preferred_element_type=jnp.float32)
        return (gate / (1.0 + jnp.exp(-gate)) * up).astype(jnp.bfloat16)

    def place(group, half, core, first, value):
        a = jnp.where(half == 0, yh, 1 - yh) * 2 + core
        rows = pl.ds(pl.multiple_of(z * 112 + first, 16), value.shape[0])
        hidden[group, a, rows, :] = value

    def block_of(groups, half, first, count, origin, core=None):
        a = jnp.where(half == 0, yh, 1 - yh) * 2
        rows = pl.ds(pl.multiple_of(lax.rem(z + origin, 8) * 112 + first, 16), count)
        return hidden.at[groups, pl.ds(a, 2) if core is None else pl.ds(a + core, 1), rows, :]

    class Spread:
        def __init__(self, index, groups, half, first, count, direct=False):
            self.index, self.where = index, (groups, half, first, count)
            places = (1, 7, 2, 6, 3, 5, 4) if direct else (1, 7, 2, 6)
            self.sent = [self.copy(i, 0, place) for i, place in enumerate(places)]
            self.direct, self.seen = direct, set()
            for copy in self.sent:
                copy.start()

        def copy(self, slot, origin, place, core=None):
            block = block_of(*self.where, origin, core)
            return remote(
                block, block, hid_s.at[self.index, slot], hid_r.at[self.index, slot], (d, s, lax.rem(z + place, 8))
            )

        def relay(self):
            for way, (origin, near, far) in enumerate(((6, 1, 2), (2, 7, 6))):
                self.sent[2 + way].wait_recv()
                more = [self.copy(4 + way, origin, near), self.copy(6 + way, origin, far, way)]
                for copy in more:
                    copy.start()
                self.sent += more

        def wait(self):
            for i, copy in enumerate(self.sent):
                if self.direct or i not in (2, 3):
                    copy.wait_recv()

    def own_units(group):
        result = units(0, slice(0, 224), tok[2 * group : 2 * group + 2].reshape(128, 4096))
        for first, count in GROUPS:
            for core in range(2):
                place(group, 0, core, first, result[2 * first + core * count : 2 * first + core * count + count])
        return Spread(group, pl.ds(group, 1), 0, 0, 112)

    def other_units(index):
        first, count = GROUPS[index]
        result = units(1, slice(first * 2, first * 2 + count * 2), tok[...].reshape(256, 4096))
        for group in range(2):
            for core in range(2):
                part = result[core * count : core * count + count, group * 128 : group * 128 + 128]
                place(group, 1, core, first, part)
        return Spread(2 + index, pl.ds(0, 2), 1, first, count, direct=index == 3)

    my_rows = rows_for(y, c)

    def ring(way, step, half):
        row = (y + 8 - step) % 8 if way == 0 else (y + step) % 8
        block = final.at[rows_for(row, c), pl.ds(half * 1792, 1792)]
        return remote(
            block, block, ring_s.at[way, step, half], ring_r.at[way, step, half], y_up if way == 0 else y_down
        )

    def ring_core(way, step, half):
        row = (y + 7 - step) % 8 if way == 0 else (y + 1 + step) % 8
        block = final.at[rows_for(row, c), pl.ds(half * 1792, 1792)]
        return remote(block, block, ringc_s.at[way, step, half], ringc_r.at[way, step, half], sib)

    def halves(way, step):
        return (0, 1) if step < 3 else (way,)

    own_piece = remote(final.at[my_rows, :], final.at[my_rows, :], own_piece_s.at[0], own_piece_r.at[0], sib)

    def ring_step(step):
        for half in range(2):
            for way in range(2):
                if half in halves(way, step):
                    ring(way, step, half).wait_recv()
                    if step < 3 and half in halves(way, step + 1):
                        ring(way, step + 1, half).start()
                    ring_core(way, step, half).start()

    def rotate():
        for part in range(4):
            sums_of = [None] * 7
            for slot, offset in enumerate((0, 1, 3, 2)):
                for block in range(7):
                    lanes = slice(block * 512 + part * 128, block * 512 + part * 128 + 128)
                    value = pieces[slot, :, lanes].astype(jnp.float32)
                    for i in range(7):
                        term = value * paley[((x + offset) % 4) * 7 + block, x * 7 + i]
                        sums_of[i] = term if sums_of[i] is None else sums_of[i] + term
            for i in range(7):
                mixed[i * 32 : i * 32 + 32, part * 128 : part * 128 + 128] = sums_of[i]
        high = mixed[...].astype(jnp.bfloat16)
        low = (mixed[...] - high.astype(jnp.float32)).astype(jnp.bfloat16)
        table = signs[...]
        rotated = jnp.dot(high, table, preferred_element_type=jnp.float32)
        rotated = (rotated + jnp.dot(low, table, preferred_element_type=jnp.float32)) * NORM
        for i in range(7):
            final[my_rows, i * 512 : i * 512 + 512] = rotated[i * 32 : i * 32 + 32].astype(jnp.bfloat16)

    steps(0, 2)
    for way in range(2):
        tok_copy(way, way).wait_recv()
        tok_forward(way).start()
    steps(2, 4)
    for copy in piece_copies:
        copy.wait_recv()
    for order in range(2):
        for way in range(2):
            gath_copy(way, way if order == 0 else 1 - way).start()
    steps(4, 6)
    wait_each(own, 0, CHUNKS)
    tok_copy(1, 0).wait_recv()
    spreads = [own_units(0)]
    steps(6, 8)
    for way in range(2):
        gath_copy(way, way).wait_recv()
        gath_forward(way).start()
    steps(8, 9)
    tok_copy(0, 1).wait_recv()
    for way in range(2):
        tok_forward(way).wait_recv()
    spreads[0].relay()
    spreads.append(own_units(1))
    steps(9, 11)
    for way in range(2):
        gath_copy(way, 1 - way).wait_recv()
        gath_forward(way).wait_recv()
    rotate()
    for half in range(2):
        for way in range(2):
            ring(way, 0, half).start()
    own_piece.start()
    steps(11, 13)
    spreads[1].relay()
    wait_each(share, 0, 2 * PARTS)
    spreads.append(other_units(0))
    steps(13, 17)
    wait_each(share, 2 * PARTS, 4 * PARTS)
    spreads.append(other_units(1))
    ring_step(0)
    spreads[2].relay()
    steps(17, 21)
    wait_each(share, 4 * PARTS, 6 * PARTS)
    spreads.append(other_units(2))
    spreads[3].relay()
    ring_step(1)
    steps(21, STEPS)
    wait_each(share, 6 * PARTS, 7 * PARTS)
    spreads.append(other_units(3))
    spreads[4].relay()
    ring_step(2)
    ring_step(3)

    own_piece.wait_recv()
    for step in range(4):
        for way in range(2):
            for half in halves(way, step):
                ring_core(way, step, half).wait_recv()

    def down(group, half):
        a = (yh if half == 0 else 1 - yh) * 2
        lanes = pl.ds(pl.multiple_of(a * 896, 128), 1792)
        block = hidden[group, pl.ds(a, 2)].reshape(1792, 128)
        return jnp.dot(final[:, lanes], block, preferred_element_type=jnp.float32)

    sum_copies = [
        remote(partial.at[pl.ds(64 * (i + 1), 64), :], sums.at[i], sum_s.at[i], sum_r.at[i], x_peers[i]) for i in range(3)
    ]
    spreads[0].wait()
    spreads[1].wait()
    for group in range(2):
        early[group] = down(group, 0)
    for spread in spreads[2:]:
        spread.wait()
    result = (early[1] + down(1, 1)).T
    partial[128:256, :] = result.astype(jnp.bfloat16)
    sum_copies[2].start()
    sum_copies[1].start()
    result = (early[0] + down(0, 1)).T
    partial[64:128, :] = result[64:].astype(jnp.bfloat16)
    sum_copies[0].start()
    total = result[:64]
    for copy in sum_copies:
        copy.wait_recv()
    for i in range(3):
        total = total + sums[i].astype(jnp.float32)
    out_ref[...] = total.astype(jnp.bfloat16)

    for copy in piece_copies + sum_copies + [own_piece]:
        copy.wait_send()
    for spread in spreads:
        for copy in spread.sent:
            copy.wait_send()
    for way in range(2):
        for half in range(2):
            tok_copy(way, half).wait_send()
            gath_copy(way, half).wait_send()
        tok_forward(way).wait_send()
        gath_forward(way).wait_send()

    def end(index, _):
        for kind in range(2):
            chain(kind, index).wait_send()
            share(kind, index).wait_send()
        return 0

    def end_own(chunk, _):
        for kind in range(2):
            own(kind, chunk).wait_send()
        return 0

    lax.fori_loop(0, CHUNKS * PARTS, end, 0)
    lax.fori_loop(0, CHUNKS, end_own, 0)
    for step in range(4):
        for way in range(2):
            for half in halves(way, step):
                ring(way, step, half).wait_send()
                ring_core(way, step, half).wait_send()


def local(tokens, gate_codes, gate_scales, up_codes, up_scales, down_codes, down_scales):
    dma = pltpu.SemaphoreType.DMA
    bf16, f32 = jnp.bfloat16, jnp.float32
    anywhere = pl.BlockSpec(memory_space=pl.ANY)
    signs = jnp.asarray(sylvester_signs(WALSH), bf16)
    paley = jnp.asarray(paley_signs())
    return pl.pallas_call(
        kernel,
        out_shape=jax.ShapeDtypeStruct((64, 512), bf16),
        in_specs=[anywhere] * 8 + [pl.BlockSpec(memory_space=pltpu.SMEM)],
        out_specs=pl.BlockSpec(memory_space=pltpu.VMEM),
        scratch_shapes=[
            pltpu.VMEM((4, 64, 4096), bf16),
            pltpu.VMEM((2, 112, 4096), bf16),
            pltpu.VMEM((2, 32, 112), f32),
            pltpu.VMEM((896, 512), bf16),
            pltpu.VMEM((7, 512), f32),
            pltpu.VMEM((512, 512), bf16),
            pltpu.VMEM((2, 2, 224, 4096), bf16),
            pltpu.VMEM((512, 896), bf16),
            pltpu.VMEM((2, 112, 32), f32),
            pltpu.VMEM((4, 32, 3584), bf16),
            pltpu.VMEM((224, 512), f32),
            pltpu.VMEM((2, 4, 896, 128), bf16),
            pltpu.VMEM((512, 3584), bf16),
            pltpu.VMEM((2, 512, 128), f32),
            pltpu.VMEM((256, 512), bf16),
            pltpu.VMEM((3, 64, 512), bf16),
            dma((8,)),
            dma((2, 2)), dma((2, 2)),
            dma((2,)), dma((2,)),
            dma((2, CHUNKS * PARTS)), dma((2, CHUNKS * PARTS)),
            dma((2, CHUNKS)), dma((2, CHUNKS)),
            dma((2, CHUNKS * PARTS)), dma((2, CHUNKS * PARTS)),
            dma((3,)), dma((3,)),
            dma((2, 2)), dma((2, 2)),
            dma((2,)), dma((2,)),
            dma((2, 4, 2)), dma((2, 4, 2)),
            dma((2, 4, 2)), dma((2, 4, 2)),
            dma((1,)), dma((1,)),
            dma((6, 8)), dma((6, 8)),
            dma((3,)), dma((3,)),
        ],
        compiler_params=pltpu.CompilerParams(
            collective_id=0, has_side_effects=True, vmem_limit_bytes=56 * 1024 * 1024
        ),
        cost_estimate=pl.CostEstimate(flops=4 * 10**9, bytes_accessed=4 * 10**6, transcendentals=10**5),
        name="feed_forward",
    )(tokens, gate_codes, gate_scales.T, up_codes, up_scales.T, down_codes, down_scales, signs, paley)


def solution(mesh):
    return jax.shard_map(
        local,
        mesh=mesh,
        in_specs=(
            P(("dp", "seq"), None),
            P(("seq", "tensor"), None),
            P(("seq", "tensor"), None),
            P(("seq", "tensor"), None),
            P(("seq", "tensor"), None),
            P("seq", "tensor"),
            P("seq", "tensor"),
        ),
        out_specs=P(("dp", "seq"), "tensor"),
        check_vma=False,
    )
```

time: 106 us -> 92.6 us (0.87)
  Pallas kernels: 102 us -> 90.9 us
  local copies, waits for them, and re-layouts: 3.64 us -> 1.47 us
    pallas_call x1, Pallas kernels: 102 us -> 90.9 us  [local(): pl.pallas_call(kernel, out_shape=jax.ShapeDtypeStruct((64, 512), bf16), i...]
    unnamed x5 -> x1, local copies, waits for them, and re-layouts: 3.64 us -> 1.47 us
where the time goes in v2:
time: 92.6 us; the launch traced here: 92.4 us
  Pallas kernels  90.9 us (98%)
  local copies, waits for them, and re-layouts  1.47 us (2%)
    pallas_call x1, Pallas kernels, local(): pl.pallas_call(kernel, out_shape=jax.ShapeDtypeStruct((64, 512), bf16), i...  90.9 us

profile of v2, /device:TPU:1, one launch (start us, length us, event | category | flops | bytes accessed | tf_op | source)
XLA Modules:
  0.0 92.4 jit_solution(7458024378803806726)
XLA Ops:
  0.0 90.9 %feed_forward.1 = bf16[64,512]{1,0:T(8,128)(2,1)} custom-call(bf16[64,4096]{1,0:T(8,128)(2,1)} %tokens_in.1, bf16[112,4096]{1,0:T(8,128)(2,1)} %gate_in.1, f32[32,112]{1,0:T(8,128)} %bitcast.2, bf16[112,4096]{1,0:T(8,128)(2,1)} %up_in.1, f32[32,112]{1,0:T(8,128)} %bitcast.3, bf16[896,512]{1,0:T(8,128)(2,1)} %down_in.1, f32[7,512]{1,0:T(8,128)} %down_scale_in.1, ...), custom_call_target="tpu_custom_call" | custom-call | flops 4000000000 | bytes 4000000 | tf_op jit(solution)/shard_map/feed_forward/pallas_call | solution.py:455
  90.9 1.5 %copy.11 = bf16[64,512]{1,0:T(8,128)(2,1)} copy(bf16[64,512]{1,0:T(8,128)(2,1)} %feed_forward.1) | data formatting | bytes 131072

commit v3 on v2

--- a/solution.py
+++ b/solution.py
@@ -50,7 +50,7 @@
     tokens_in, gate_in, gate_scale_in, up_in, up_scale_in, down_in, down_scale_in, signs_in, paley,
     out_ref,
     tok, codes, scales, dcodes, dscales, signs, weights, turned, turned_scales, pieces, mixed, hidden, final, early, partial, sums,
-    load_sem, tok_s, tok_r, tokf_s, tokf_r, chain_s, chain_r, own_s, own_r, share_s, share_r, piece_s, piece_r, gath_s, gath_r, gathf_s, gathf_r,
+    load_sem, tok_s, tok_r, tokf_s, tokf_r, chain_s, chain_r, own_s, own_r, share_s, share_r, piece_s, piece_r, gath_s, gath_r,
     ring_s, ring_r, ringc_s, ringc_r, own_piece_s, own_piece_r, hid_s, hid_r, sum_s, sum_r,
 ):
     d, s, z = lax.axis_index("dp"), lax.axis_index("seq"), lax.axis_index("tensor")
@@ -87,7 +87,6 @@
     peers = [sib, *x_peers, *z_peers, y_up, y_down, opp, opp_sib]
     for peer in peers:
         pl.semaphore_signal(barrier, inc=1, device_id=peer, device_id_type=MESH)
-    pl.semaphore_wait(barrier, len(peers))
 
     x_up, x_down, x_far = x_peers
 
@@ -101,23 +100,12 @@
         rows = pl.ds(way * 32, 32)
         return remote(tok.at[2 - way, rows], tok.at[3, rows], tokf_s.at[way], tokf_r.at[way], (x_up, x_down)[way])
 
-    def gath_copy(way, half):
-        rows = pl.ds(half * 16, 16)
+    def gath_copy(half, peer):
+        lanes = pl.ds(pl.multiple_of(jnp.where(half == 0, yh, 1 - yh) * 1792, 128), 1792)
         return remote(
-            pieces.at[0, rows], pieces.at[2 - way, rows], gath_s.at[way, half], gath_r.at[way, half],
-            (x_up, x_down)[way],
-        )
-
-    def gath_forward(way):
-        rows = pl.ds(way * 16, 16)
-        return remote(
-            pieces.at[2 - way, rows], pieces.at[3, rows], gathf_s.at[way], gathf_r.at[way], (x_up, x_down)[way]
-        )
-
-    loads[0].wait()
-    for order in range(2):
-        for way in range(2):
-            tok_copy(way, way if order == 0 else 1 - way).start()
+            pieces.at[0, :, lanes], pieces.at[(2, 1, 3)[peer], :, lanes],
+            gath_s.at[half, peer], gath_r.at[half, peer], x_peers[peer],
+        )
 
     for load in loads[5:]:
         load.wait()
@@ -137,8 +125,6 @@
             [(rows_for(y, 1 - c), sib), (rows_for(y_opp, c), opp), (rows_for(y_opp, 1 - c), opp_sib)]
         )
     ]
-    for copy in piece_copies:
-        copy.start()
     pieces[0, :, own_lanes] = turned[rows_for(y, c), :]
 
     for load in loads[1:5]:
@@ -179,16 +165,33 @@
                 lanes = slice(group * 128, group * 128 + 128)
                 value = codes[kind, pl.ds(at, 16), lanes].astype(jnp.float32) * scale[:, group : group + 1]
                 weights[kind, 0, pl.ds(row, 16), lanes] = value.astype(jnp.bfloat16)
+        return 0
+
+    lax.fori_loop(0, CHUNKS, expand, 0)
+    loads[0].wait()
+
+    pl.semaphore_wait(barrier, len(peers))
+    for copy in piece_copies:
+        copy.start()
+    for way in range(2):
+        tok_copy(way, way).start()
+
+    def first_hop(index, _):
+        for kind in range(2):
 
             @pl.when(d == (3 if kind == 0 else 0))
             def _():
-                for part in range(PARTS):
-                    chain(kind, chunk * PARTS + part).start()
-
+                chain(kind, index).start()
+
+        return 0
+
+    def to_core(chunk, _):
+        for kind in range(2):
             own(kind, chunk).start()
         return 0
 
-    lax.fori_loop(0, CHUNKS, expand, 0)
+    lax.fori_loop(0, CHUNKS * PARTS, first_hop, 0)
+    lax.fori_loop(0, CHUNKS, to_core, 0)
 
     def steps(first, end):
         def body(n, _):
@@ -261,11 +264,14 @@
                 if self.direct or i not in (2, 3):
                     copy.wait_recv()
 
-    def own_units(group):
-        result = units(0, slice(0, 224), tok[2 * group : 2 * group + 2].reshape(128, 4096))
-        for first, count in GROUPS:
-            for core in range(2):
-                place(group, 0, core, first, result[2 * first + core * count : 2 * first + core * count + count])
+    def own_units(group, index):
+        first, count = GROUPS[index]
+        lane_tokens = tok[2 * group : 2 * group + 2].reshape(128, 4096)
+        result = units(0, slice(first * 2, first * 2 + count * 2), lane_tokens)
+        for core in range(2):
+            place(group, 0, core, first, result[core * count : core * count + count])
+
+    def own_spread(group):
         return Spread(group, pl.ds(group, 1), 0, 0, 112)
 
     def other_units(index):
@@ -305,18 +311,19 @@
                         ring(way, step + 1, half).start()
                     ring_core(way, step, half).start()
 
+    def mix(part):
+        sums_of = [None] * 7
+        for slot, offset in enumerate((0, 1, 3, 2)):
+            for block in range(7):
+                lanes = slice(block * 512 + part * 128, block * 512 + part * 128 + 128)
+                value = pieces[slot, :, lanes].astype(jnp.float32)
+                for i in range(7):
+                    term = value * paley[((x + offset) % 4) * 7 + block, x * 7 + i]
+                    sums_of[i] = term if sums_of[i] is None else sums_of[i] + term
+        for i in range(7):
+            mixed[i * 32 : i * 32 + 32, part * 128 : part * 128 + 128] = sums_of[i]
+
     def rotate():
-        for part in range(4):
-            sums_of = [None] * 7
-            for slot, offset in enumerate((0, 1, 3, 2)):
-                for block in range(7):
-                    lanes = slice(block * 512 + part * 128, block * 512 + part * 128 + 128)
-                    value = pieces[slot, :, lanes].astype(jnp.float32)
-                    for i in range(7):
-                        term = value * paley[((x + offset) % 4) * 7 + block, x * 7 + i]
-                        sums_of[i] = term if sums_of[i] is None else sums_of[i] + term
-            for i in range(7):
-                mixed[i * 32 : i * 32 + 32, part * 128 : part * 128 + 128] = sums_of[i]
         high = mixed[...].astype(jnp.bfloat16)
         low = (mixed[...] - high.astype(jnp.float32)).astype(jnp.bfloat16)
         table = signs[...]
@@ -325,58 +332,79 @@
         for i in range(7):
             final[my_rows, i * 512 : i * 512 + 512] = rotated[i * 32 : i * 32 + 32].astype(jnp.bfloat16)
 
+    spreads = [None] * 6
+    piece_copies[0].wait_recv()
+    for peer in (2, 0, 1):
+        gath_copy(0, peer).start()
     steps(0, 2)
+    piece_copies[1].wait_recv()
+    piece_copies[2].wait_recv()
+    for peer in (2, 0, 1):
+        gath_copy(1, peer).start()
+    for way in range(2):
+        tok_copy(way, 1 - way).start()
+    steps(2, 5)
     for way in range(2):
         tok_copy(way, way).wait_recv()
         tok_forward(way).start()
-    steps(2, 4)
-    for copy in piece_copies:
-        copy.wait_recv()
-    for order in range(2):
-        for way in range(2):
-            gath_copy(way, way if order == 0 else 1 - way).start()
-    steps(4, 6)
-    wait_each(own, 0, CHUNKS)
-    tok_copy(1, 0).wait_recv()
-    spreads = [own_units(0)]
-    steps(6, 8)
-    for way in range(2):
-        gath_copy(way, way).wait_recv()
-        gath_forward(way).start()
-    steps(8, 9)
-    tok_copy(0, 1).wait_recv()
-    for way in range(2):
-        tok_forward(way).wait_recv()
-    spreads[0].relay()
-    spreads.append(own_units(1))
-    steps(9, 11)
-    for way in range(2):
-        gath_copy(way, 1 - way).wait_recv()
-        gath_forward(way).wait_recv()
+    steps(5, 7)
+    for half in range(2):
+        for peer in range(3):
+            gath_copy(half, peer).wait_recv()
+    mix(0)
+    mix(1)
+    steps(7, 8)
+    mix(2)
+    mix(3)
     rotate()
     for half in range(2):
         for way in range(2):
             ring(way, 0, half).start()
     own_piece.start()
+    wait_each(own, 0, CHUNKS)
+    tok_copy(1, 0).wait_recv()
+    own_units(0, 0)
+    steps(8, 9)
+    own_units(0, 1)
+    steps(9, 10)
+    own_units(0, 2)
+    steps(10, 11)
+    own_units(0, 3)
+    spreads[0] = own_spread(0)
     steps(11, 13)
+    tok_copy(0, 1).wait_recv()
+    for way in range(2):
+        tok_forward(way).wait_recv()
+    own_units(1, 0)
+    steps(13, 14)
+    own_units(1, 1)
+    spreads[0].relay()
+    steps(14, 15)
+    own_units(1, 2)
+    steps(15, 16)
+    own_units(1, 3)
+    spreads[1] = own_spread(1)
+    ring_step(0)
+    steps(16, 17)
+    wait_each(share, 0 * PARTS, 2 * PARTS)
+    spreads[2] = other_units(0)
+    steps(17, 18)
     spreads[1].relay()
-    wait_each(share, 0, 2 * PARTS)
-    spreads.append(other_units(0))
-    steps(13, 17)
+    steps(18, 19)
     wait_each(share, 2 * PARTS, 4 * PARTS)
-    spreads.append(other_units(1))
-    ring_step(0)
+    spreads[3] = other_units(1)
     spreads[2].relay()
-    steps(17, 21)
+    steps(19, 20)
+    ring_step(1)
+    steps(20, 21)
     wait_each(share, 4 * PARTS, 6 * PARTS)
-    spreads.append(other_units(2))
+    spreads[4] = other_units(2)
     spreads[3].relay()
-    ring_step(1)
-    steps(21, STEPS)
+    steps(21, 23)
     wait_each(share, 6 * PARTS, 7 * PARTS)
-    spreads.append(other_units(3))
+    spreads[5] = other_units(3)
+    ring_step(2)
     spreads[4].relay()
-    ring_step(2)
     ring_step(3)
 
     own_piece.wait_recv()
@@ -422,9 +450,9 @@
     for way in range(2):
         for half in range(2):
             tok_copy(way, half).wait_send()
-            gath_copy(way, half).wait_send()
         tok_forward(way).wait_send()
-        gath_forward(way).wait_send()
+        for peer in range(3):
+            gath_copy(way, peer).wait_send()
 
     def end(index, _):
         for kind in range(2):
@@ -481,8 +509,7 @@
             dma((2, CHUNKS)), dma((2, CHUNKS)),
             dma((2, CHUNKS * PARTS)), dma((2, CHUNKS * PARTS)),
             dma((3,)), dma((3,)),
-            dma((2, 2)), dma((2, 2)),
-            dma((2,)), dma((2,)),
+            dma((2, 3)), dma((2, 3)),
             dma((2, 4, 2)), dma((2, 4, 2)),
             dma((2, 4, 2)), dma((2, 4, 2)),
             dma((1,)), dma((1,)),

time: 92.6 us -> 89.2 us (0.963)
  Pallas kernels: 90.9 us -> 87.5 us
    pallas_call x1, Pallas kernels: 90.9 us -> 87.5 us  [local(): pl.pallas_call(kernel, out_shape=jax.ShapeDtypeStruct((64, 512), bf16), i...]
where the time goes in v3:
time: 89.2 us; the launch traced here: 89 us
  Pallas kernels  87.5 us (98%)
  local copies, waits for them, and re-layouts  1.47 us (2%)
    pallas_call x1, Pallas kernels, local(): pl.pallas_call(kernel, out_shape=jax.ShapeDtypeStruct((64, 512), bf16), i...  87.5 us

profile of v3, /device:TPU:1, one launch (start us, length us, event | category | flops | bytes accessed | tf_op | source)
XLA Modules:
  0.0 89.0 jit_solution(15119763634034062486)
XLA Ops:
  0.0 87.5 %feed_forward.1 = bf16[64,512]{1,0:T(8,128)(2,1)} custom-call(bf16[64,4096]{1,0:T(8,128)(2,1)} %tokens_in.1, bf16[112,4096]{1,0:T(8,128)(2,1)} %gate_in.1, f32[32,112]{1,0:T(8,128)} %bitcast.2, bf16[112,4096]{1,0:T(8,128)(2,1)} %up_in.1, f32[32,112]{1,0:T(8,128)} %bitcast.3, bf16[896,512]{1,0:T(8,128)(2,1)} %down_in.1, f32[7,512]{1,0:T(8,128)} %down_scale_in.1, ...), custom_call_target="tpu_custom_call" | custom-call | flops 4000000000 | bytes 4000000 | tf_op jit(solution)/shard_map/feed_forward/pallas_call | solution.py:483
  87.5 1.5 %copy.11 = bf16[64,512]{1,0:T(8,128)(2,1)} copy(bf16[64,512]{1,0:T(8,128)(2,1)} %feed_forward.1) | data formatting | bytes 131072

commit v4 on v3

--- a/solution.py
+++ b/solution.py
@@ -353,7 +353,6 @@
             gath_copy(half, peer).wait_recv()
     mix(0)
     mix(1)
-    steps(7, 8)
     mix(2)
     mix(3)
     rotate()
@@ -361,6 +360,7 @@
         for way in range(2):
             ring(way, 0, half).start()
     own_piece.start()
+    steps(7, 8)
     wait_each(own, 0, CHUNKS)
     tok_copy(1, 0).wait_recv()
     own_units(0, 0)
@@ -401,9 +401,9 @@
     spreads[4] = other_units(2)
     spreads[3].relay()
     steps(21, 23)
+    ring_step(2)
     wait_each(share, 6 * PARTS, 7 * PARTS)
     spreads[5] = other_units(3)
-    ring_step(2)
     spreads[4].relay()
     ring_step(3)
 

time: 89.2 us -> 88.9 us (level)
  the two profiles are of different devices: /device:TPU:1 before, /device:TPU:64 now
where the time goes in v4:
time: 88.9 us; the launch traced here: 88.7 us
  Pallas kernels  87.2 us (98%)
  local copies, waits for them, and re-layouts  1.47 us (2%)
    pallas_call x1, Pallas kernels, local(): pl.pallas_call(kernel, out_shape=jax.ShapeDtypeStruct((64, 512), bf16), i...  87.2 us

profile of v4, /device:TPU:64, one launch (start us, length us, event | category | flops | bytes accessed | tf_op | source)
XLA Modules:
  0.0 88.7 jit_solution(4670541899001895116)
XLA Ops:
  0.0 87.2 %feed_forward.1 = bf16[64,512]{1,0:T(8,128)(2,1)} custom-call(bf16[64,4096]{1,0:T(8,128)(2,1)} %tokens_in.1, bf16[112,4096]{1,0:T(8,128)(2,1)} %gate_in.1, f32[32,112]{1,0:T(8,128)} %bitcast.2, bf16[112,4096]{1,0:T(8,128)(2,1)} %up_in.1, f32[32,112]{1,0:T(8,128)} %bitcast.3, bf16[896,512]{1,0:T(8,128)(2,1)} %down_in.1, f32[7,512]{1,0:T(8,128)} %down_scale_in.1, ...), custom_call_target="tpu_custom_call" | custom-call | flops 4000000000 | bytes 4000000 | tf_op jit(solution)/shard_map/feed_forward/pallas_call | solution.py:483
  87.2 1.5 %copy.11 = bf16[64,512]{1,0:T(8,128)(2,1)} copy(bf16[64,512]{1,0:T(8,128)(2,1)} %feed_forward.1) | data formatting | bytes 131072
